TPU v7x, 32 devices: a whole 2x2x4 slice. The times are simulated.
32 devices in a mesh: dp: 8 (over z, x), seq: 4 (over y, core).
Axes of the slice: x: 2, y: 2, z: 4, core: 2. Of those that a mesh axis runs over, the one named last changes fastest.
Arguments:
- hidden_states: bfloat16 [8, 512, 4096], P('dp', 'seq'), may hold values from -6 to 6
- queries: bfloat16 [8, 512, 4096], P('dp', 'seq'), may hold values from -20 to 20
- key_states: bfloat16 [8, 512, 512], P('dp', 'seq'), may hold values from -6 to 6
- context_grad: bfloat16 [8, 512, 4096], P('dp', 'seq'), may hold values from -6 to 6
- doc_lengths: int32 [8, 16], P('dp'), may hold values from 1 to 64, 512 in all within a row
- value_weight: bfloat16 [4096, 512], P('dp'), may hold values from -0.09375 to 0.09375
Outputs:
- hidden_grad: bfloat16 [8, 512, 4096], P('dp', 'seq')
- query_grad: bfloat16 [8, 512, 4096], P('dp', 'seq')
- key_grad: bfloat16 [8, 512, 512], P('dp', 'seq')
- value_weight_grad: float32 [4096, 512], P(('dp', 'seq'))
Inputs may be any that keep to these rules, and one draw needn't show every extreme that they name: `doc_lengths`: row s holds the lengths of the 16 documents of sequence s in order; they sum to 512.
All inputs are finite; a program needn't handle non-finite values.
Results may differ from a plain program's by a relative error of at most 0.011.
Values may be sent and summed in bfloat16 or wider, within the bound.
A program may use at most 128 MiB of HBM per device.

v0:
```python
import jax
import jax.numpy as jnp
from jax import lax
from jax.sharding import PartitionSpec as P

HD = 128
far_negative = -1e30


def segment_ids(lengths_row, length):
    doc_ends = jnp.cumsum(lengths_row)
    positions = jnp.arange(length, dtype=jnp.int32)
    return jnp.sum((positions[:, None] >= doc_ends[None, :]).astype(jnp.int32), axis=1)


def attend(query_all, key_all, value_all, grad_all, segment):
    length, head_count, head_width = query_all.shape
    row_block = min(length, max(512, length // 8))
    longest_doc = length // 8
    score_scale = head_width ** (-0.5)
    positions = jnp.arange(length, dtype=jnp.int32)
    key_acc = jnp.zeros((length, head_count, head_width), jnp.float32)
    value_acc = jnp.zeros((length, head_count, head_width), jnp.float32)
    query_parts = []
    for row_start in range(0, length, row_block):
        row_end = row_start + row_block
        key_start = max(0, row_start - longest_doc)
        query_rows = query_all[row_start:row_end]
        grad_rows = grad_all[row_start:row_end]
        key_rows = key_all[key_start:row_end]
        value_rows = value_all[key_start:row_end]
        allowed = (positions[None, key_start:row_end] <= positions[row_start:row_end, None]) & (
            segment[None, key_start:row_end] == segment[row_start:row_end, None]
        )
        scores = (
            jnp.einsum("ihd,jhd->hij", query_rows, key_rows, preferred_element_type=jnp.float32)
            * score_scale
        )
        scores = jnp.where(allowed[None], scores, far_negative)
        row_peak = jnp.max(scores, axis=-1, keepdims=True)
        exponent = jnp.exp(scores - row_peak)
        softmax_weights = exponent / jnp.sum(exponent, axis=-1, keepdims=True)
        weights_low = softmax_weights.astype(jnp.bfloat16)
        attended = jnp.einsum(
            "hij,jhd->ihd", weights_low, value_rows, preferred_element_type=jnp.float32
        )
        row_delta = jnp.sum(grad_rows.astype(jnp.float32) * attended, axis=-1)
        softmax_grad = jnp.einsum(
            "ihd,jhd->hij", grad_rows, value_rows, preferred_element_type=jnp.float32
        )
        score_grad = softmax_weights * (softmax_grad - jnp.transpose(row_delta)[:, :, None])
        score_low = score_grad.astype(jnp.bfloat16)
        query_parts.append(
            (
                jnp.einsum("hij,jhd->ihd", score_low, key_rows, preferred_element_type=jnp.float32)
                * score_scale
            ).astype(jnp.bfloat16)
        )
        key_acc = key_acc.at[key_start:row_end].add(
            jnp.einsum("hij,ihd->jhd", score_low, query_rows, preferred_element_type=jnp.float32)
            * score_scale
        )
        value_acc = value_acc.at[key_start:row_end].add(
            jnp.einsum("hij,ihd->jhd", weights_low, grad_rows, preferred_element_type=jnp.float32)
        )
    return (jnp.concatenate(query_parts, axis=0), key_acc, value_acc)


def body(hidden_states, queries, key_states, context_grad, doc_lengths, value_weight):
    tokens = hidden_states.shape[1]
    rows_here = hidden_states[0]
    heads_total = queries.shape[2] // HD
    kv_heads = key_states.shape[2] // HD
    group_size = heads_total // kv_heads
    columns = rows_here
    values = jnp.dot(
        columns,
        lax.all_gather(value_weight, "dp", axis=0, tiled=True),
        preferred_element_type=jnp.float32,
    ).astype(jnp.bfloat16)
    query_heads = queries[0].reshape(tokens, heads_total, HD)
    grad_heads = context_grad[0].reshape(tokens, heads_total, HD)
    query_all, grad_all = (
        lax.all_to_all(query_heads, "seq", split_axis=1, concat_axis=0, tiled=True),
        lax.all_to_all(grad_heads, "seq", split_axis=1, concat_axis=0, tiled=True),
    )
    length = query_all.shape[0]
    key_three = key_states[0].reshape(tokens, kv_heads, HD)
    value_three = values.reshape(tokens, kv_heads, HD)
    segment = segment_ids(doc_lengths[0], length)
    key_all, value_all = (
        lax.all_to_all(
            jnp.repeat(key_three, group_size, axis=1),
            "seq",
            split_axis=1,
            concat_axis=0,
            tiled=True,
        ),
        lax.all_to_all(
            jnp.repeat(value_three, group_size, axis=1),
            "seq",
            split_axis=1,
            concat_axis=0,
            tiled=True,
        ),
    )
    query_back, key_back, value_back = attend(query_all, key_all, value_all, grad_all, segment)
    key_home, value_home = (
        lax.all_to_all(
            key_back.astype(jnp.bfloat16), "seq", split_axis=0, concat_axis=1, tiled=True
        ).astype(key_back.dtype),
        lax.all_to_all(
            value_back.astype(jnp.bfloat16), "seq", split_axis=0, concat_axis=1, tiled=True
        ).astype(value_back.dtype),
    )
    key_sum = jnp.sum(key_home.reshape(tokens, kv_heads, group_size, HD), axis=2)
    value_sum = jnp.sum(value_home.reshape(tokens, kv_heads, group_size, HD), axis=2)
    query_home = lax.all_to_all(query_back, "seq", split_axis=0, concat_axis=1, tiled=True)
    value_low = value_sum.reshape(tokens, kv_heads * HD).astype(jnp.bfloat16)
    hidden_grad = jnp.einsum(
        "tc,rc->tr",
        value_low,
        lax.all_gather(value_weight, "dp", axis=0, tiled=True),
        preferred_element_type=jnp.float32,
    )
    columns = rows_here
    weight_grad = lax.psum_scatter(
        jnp.einsum("tr,tc->rc", columns, value_low, preferred_element_type=jnp.float32),
        ("dp", "seq"),
        scatter_dimension=0,
        tiled=True,
    )
    return (
        hidden_grad.astype(jnp.bfloat16)[None],
        query_home.reshape(tokens, heads_total * HD)[None],
        key_sum.reshape(tokens, kv_heads * HD).astype(jnp.bfloat16)[None],
        weight_grad,
    )


def solution(mesh):
    return jax.shard_map(
        body,
        mesh=mesh,
        in_specs=(
            P("dp", "seq", None),
            P("dp", "seq", None),
            P("dp", "seq", None),
            P("dp", "seq", None),
            P("dp", None),
            P("dp", None),
        ),
        out_specs=(
            P("dp", "seq", None),
            P("dp", "seq", None),
            P("dp", "seq", None),
            P(("dp", "seq"), None),
        ),
        check_vma=False,
    )
```

profile of v0, /device:TPU:0, one launch (start us, length us, event | category | flops | bytes accessed | tf_op | source)
XLA Modules:
  0.0 270.5 jit_solution(17113018626907057216)
XLA Ops:
  11.7 4.2 %all-to-all-start = ((bf16[128,32,128]{2,0,1:T(8,128)(2,1)}), bf16[128,32,128]{2,0,1:T(8,128)(2,1)S(1)}, u32[]{:S(2)}, u32[]{:S(2)}) async-start(bf16[128,32,128]{2,0,1:T(8,128)(2,1)} %copy.94), calls=%async_computation | async-start | bytes 2097152 | tf_op jit(solution)/shard_map/all_to_all | solution.py:84
  16.0 14.4 %all-to-all-done = bf16[128,32,128]{2,0,1:T(8,128)(2,1)S(1)} async-done(((bf16[128,32,128]{2,0,1:T(8,128)(2,1)}), bf16[128,32,128]{2,0,1:T(8,128)(2,1)S(1)}, u32[]{:S(2)}, u32[]{:S(2)}) %all-to-all-start) | async-done | bytes 1048608 | tf_op jit(solution)/shard_map/all_to_all | solution.py:84
  31.6 3.7 %all-to-all-start.1 = ((bf16[128,32,128]{2,0,1:T(8,128)(2,1)}), bf16[128,32,128]{2,0,1:T(8,128)(2,1)S(1)}, u32[]{:S(2)}, u32[]{:S(2)}) async-start(bf16[128,32,128]{2,0,1:T(8,128)(2,1)} %bitcast.84), calls=%async_computation.1 | async-start | bytes 2097152 | tf_op jit(solution)/shard_map/all_to_all | solution.py:92
  35.3 2.3 copy.100
  37.5 2.3 copy.101
  39.8 9.9 %all-to-all-done.1 = bf16[128,32,128]{2,0,1:T(8,128)(2,1)S(1)} async-done(((bf16[128,32,128]{2,0,1:T(8,128)(2,1)}), bf16[128,32,128]{2,0,1:T(8,128)(2,1)S(1)}, u32[]{:S(2)}, u32[]{:S(2)}) %all-to-all-start.1) | async-done | bytes 1048608 | tf_op jit(solution)/shard_map/all_to_all | solution.py:92
  49.7 4.2 %all-to-all-start.2 = ((bf16[128,32,128]{2,0,1:T(8,128)(2,1)}), bf16[128,32,128]{2,0,1:T(8,128)(2,1)}, u32[]{:S(2)}, u32[]{:S(2)}) async-start(bf16[128,32,128]{2,0,1:T(8,128)(2,1)} %copy.101), calls=%async_computation.2 | async-start | bytes 2097152 | tf_op jit(solution)/shard_map/all_to_all | solution.py:85
  56.6 11.8 %all-to-all-done.2 = bf16[128,32,128]{2,0,1:T(8,128)(2,1)} async-done(((bf16[128,32,128]{2,0,1:T(8,128)(2,1)}), bf16[128,32,128]{2,0,1:T(8,128)(2,1)}, u32[]{:S(2)}, u32[]{:S(2)}) %all-to-all-start.2) | async-done | bytes 1048608 | tf_op jit(solution)/shard_map/all_to_all | solution.py:85
  69.8 7.5 %fusion.20 = (f32[8,512]{1,0:T(8,128)S(1)}, f32[8,512,512]{1,2,0:T(8,128)}) fusion(pred[512,512]{0,1:T(8,128)(4,1)S(1)} %fusion.15, bf16[512,8,128]{2,0,1:T(8,128)(2,1)S(1)} %bitcast.96, bf16[512,8,128]{2,0,1:T(8,128)(2,1)} %bitcast.98), kind=kOutput, calls=%fused_computation.34 | convolution fusion | flops 545260032 | bytes 10764288 | tf_op jit(solution)/shard_map/sub | solution.py:41
  77.3 4.6 %fusion.7 = bf16[8,512,512]{1,2,0:T(8,128)(2,1)S(1)} fusion(f32[8,512,512]{1,2,0:T(8,128)} %get-tuple-element.69, f32[8,512]{1,0:T(8,128)S(1)} %get-tuple-element.68), kind=kLoop, calls=%fused_computation.13 | loop fusion | flops 4194304 | bytes 12599296 | tf_op jit(solution)/shard_map/convert_element_type | solution.py:43
  83.9 16.9 %all_to_all.105 = bf16[512,8,128]{2,1,0:T(8,128)(2,1)S(1)} all-to-all(bf16[512,8,128]{2,1,0:T(8,128)(2,1)S(1)} %copy.104), channel_id=1, replica_groups=mesh['dp'=8,'seq'=4] {'seq'}, dimensions={0} | all-to-all | bytes 2097152 | tf_op jit(solution)/shard_map/all_to_all | solution.py:112
  101.6 4.5 %convolution_bitcast_fusion = f32[4096,512]{0,1:T(8,128)} fusion(bf16[128,512]{0,1:T(8,128)(2,1)S(1)} %bitcast.94, bf16[1,128,4096]{2,1,0:T(8,128)(2,1)S(1)} %copy-done), kind=kOutput, calls=%fused_computation.5 | convolution fusion | flops 536870912 | bytes 9568256 | tf_op jit(solution)/shard_map/tr,tc->rc/dot_general | solution.py:128
  106.2 3.1 %fusion.12 = bf16[16,4,8,128]{3,2,1,0:T(8,128)(2,1)S(1)} fusion(bf16[4096,512]{1,0:T(8,128)(2,1)} %all-gather.2.cloned.1.call-done, bf16[1,128,4096]{2,1,0:T(8,128)(2,1)S(1)} %copy-done), kind=kOutput, calls=%fused_computation.23 | convolution fusion | flops 536936448 | bytes 5373952 | tf_op jit(solution)/shard_map/dot_general | solution.py:76
  109.5 28.8 %all_to_all.106 = bf16[128,32,128]{2,0,1:T(8,128)(2,1)S(1)} all-to-all(bf16[128,32,128]{2,0,1:T(8,128)(2,1)S(1)} %bitcast.85), channel_id=1, replica_groups=mesh['dp'=8,'seq'=4] {'seq'}, dimensions={1} | all-to-all | bytes 2097152 | tf_op jit(solution)/shard_map/all_to_all | solution.py:99
  140.2 4.8 %fusion.1 = bf16[8,512,512]{1,2,0:T(8,128)(2,1)S(1)} fusion(f32[8,512]{1,0:T(8,128)S(1)} %bitcast.104, f32[8,512,512]{1,2,0:T(8,128)} %get-tuple-element.69, f32[8,512]{1,0:T(8,128)S(1)} %get-tuple-element.68, bf16[512,8,128]{2,0,1:T(8,128)(2,1)S(1)} %bitcast.93, bf16[512,8,128]{2,0,1:T(8,128)(2,1)S(1)} %bitcast.91), kind=kOutput, calls=%fused_computation.2 | convolution fusion | flops 545259520 | bytes 14712832 | tf_op jit(solution)/shard_map/ihd,jhd->hij/dot_general | solution.py:48
  148.6 3.5 %all-to-all-start.5 = ((bf16[512,8,128]{2,1,0:T(8,128)(2,1)}), bf16[512,8,128]{2,1,0:T(8,128)(2,1)S(1)}, u32[]{:S(2)}, u32[]{:S(2)}) async-start(bf16[512,8,128]{2,1,0:T(8,128)(2,1)} %copy.113), calls=%async_computation.5 | async-start | bytes 2097152 | tf_op jit(solution)/shard_map/all_to_all | solution.py:118
  152.1 3.5 %fusion.11 = bf16[512,8,128]{2,0,1:T(8,128)(2,1)S(1)} fusion(bf16[8,512,512]{1,2,0:T(8,128)(2,1)} %copy-done.8, bf16[512,8,128]{2,0,1:T(8,128)(2,1)S(1)} %bitcast.97), kind=kOutput, calls=%fused_computation.21 | convolution fusion | flops 537919488 | bytes 6291456 | tf_op jit(solution)/shard_map/hij,ihd->jhd/dot_general | solution.py:60
  157.4 21.1 %all-to-all-done.5 = bf16[512,8,128]{2,1,0:T(8,128)(2,1)S(1)} async-done(((bf16[512,8,128]{2,1,0:T(8,128)(2,1)}), bf16[512,8,128]{2,1,0:T(8,128)(2,1)S(1)}, u32[]{:S(2)}, u32[]{:S(2)}) %all-to-all-start.5) | async-done | bytes 1048608 | tf_op jit(solution)/shard_map/all_to_all | solution.py:118
  178.4 3.5 %all-to-all-start.6 = ((bf16[512,8,128]{2,1,0:T(8,128)(2,1)}), bf16[512,8,128]{2,1,0:T(8,128)(2,1)S(1)}, u32[]{:S(2)}, u32[]{:S(2)}) async-start(bf16[512,8,128]{2,1,0:T(8,128)(2,1)} %copy.115), calls=%async_computation.6 | async-start | bytes 2097152 | tf_op jit(solution)/shard_map/all_to_all | solution.py:109
  181.9 4.7 %fusion.3 = bf16[1,128,4096]{2,1,0:T(8,128)(2,1)} fusion(bf16[128,512]{0,1:T(8,128)(2,1)S(1)} %bitcast.95, bf16[4096,512]{1,0:T(8,128)(2,1)} %all-gather.2.cloned.1.call-done), kind=kOutput, calls=%fused_computation.8 | convolution fusion | flops 537395200 | bytes 5373952 | tf_op jit(solution)/shard_map/tc,rc->tr/dot_general | solution.py:120
  187.8 2.3 broadcast_in_dim_reshape.3
  190.1 18.4 %all-to-all-done.6 = bf16[512,8,128]{2,1,0:T(8,128)(2,1)S(1)} async-done(((bf16[512,8,128]{2,1,0:T(8,128)(2,1)}), bf16[512,8,128]{2,1,0:T(8,128)(2,1)S(1)}, u32[]{:S(2)}, u32[]{:S(2)}) %all-to-all-start.6) | async-done | bytes 1048608 | tf_op jit(solution)/shard_map/all_to_all | solution.py:109
  210.1 51.2 %reduce-scatter.2.cloned.1.call-done = f32[128,512]{0,1:T(8,128)} async-done(((f32[4096,512]{0,1:T(8,128)}), f32[128,512]{0,1:T(8,128)}) %reduce-scatter.2.cloned.1.call-update) | async-done | bytes 262160 | tf_op jit(solution)/shard_map/reduce_scatter | solution.py:127
  261.3 1.8 copy.118
  (51 shorter events, 21.9 us)
Async XLA Ops:
  8.0 93.6 %copy-start = (bf16[1,128,4096]{2,1,0:T(8,128)(2,1)S(1)}, bf16[1,128,4096]{2,1,0:T(8,128)(2,1)}, u32[]{:S(2)}) copy-start(bf16[1,128,4096]{2,1,0:T(8,128)(2,1)} %param.14) | copy-start | bytes 3145732
  8.0 7.9 %copy-start.6 = (bf16[1,128,512]{2,1,0:T(8,128)(2,1)S(1)}, bf16[1,128,512]{2,1,0:T(8,128)(2,1)}, u32[]{:S(2)}) copy-start(bf16[1,128,512]{2,1,0:T(8,128)(2,1)} %param.16) | copy-start | bytes 393220
  8.0 98.1 %all-gather.2.cloned.1.call-start = ((), (), s32[]{:S(2)}) async-start(), calls=%async_computation.8 | async-start | bytes 4718592 | tf_op jit(solution)/shard_map/all_gather | solution.py:123
  11.7 18.7 %all-to-all-start = ((bf16[128,32,128]{2,0,1:T(8,128)(2,1)}), bf16[128,32,128]{2,0,1:T(8,128)(2,1)S(1)}, u32[]{:S(2)}, u32[]{:S(2)}) async-start(bf16[128,32,128]{2,0,1:T(8,128)(2,1)} %copy.94), calls=%async_computation | async-start | bytes 2097152 | tf_op jit(solution)/shard_map/all_to_all | solution.py:84
  31.6 22.4 %copy-start.7 = (s32[1,16]{1,0:T(1,128)S(1)}, s32[1,16]{1,0:T(1,128)}, u32[]{:S(2)}) copy-start(s32[1,16]{1,0:T(1,128)} %param.18) | copy-start | bytes 196
  31.6 18.1 %all-to-all-start.1 = ((bf16[128,32,128]{2,0,1:T(8,128)(2,1)}), bf16[128,32,128]{2,0,1:T(8,128)(2,1)S(1)}, u32[]{:S(2)}, u32[]{:S(2)}) async-start(bf16[128,32,128]{2,0,1:T(8,128)(2,1)} %bitcast.84), calls=%async_computation.1 | async-start | bytes 2097152 | tf_op jit(solution)/shard_map/all_to_all | solution.py:92
  49.7 18.8 %all-to-all-start.2 = ((bf16[128,32,128]{2,0,1:T(8,128)(2,1)}), bf16[128,32,128]{2,0,1:T(8,128)(2,1)}, u32[]{:S(2)}, u32[]{:S(2)}) async-start(bf16[128,32,128]{2,0,1:T(8,128)(2,1)} %copy.101), calls=%async_computation.2 | async-start | bytes 2097152 | tf_op jit(solution)/shard_map/all_to_all | solution.py:85
  53.9 207.4 %reduce-scatter.2.cloned.1.call-start = ((), (), s32[]{:S(2)}) async-start(), calls=%async_computation.9 | async-start | bytes 8650752 | tf_op jit(solution)/shard_map/reduce_scatter | solution.py:127
  55.6 14.2 %copy-start.3 = (bf16[4,128,8,128]{3,1,0,2:T(8,128)(2,1)S(1)}, bf16[4,128,8,128]{3,1,0,2:T(8,128)(2,1)}, u32[]{:S(2)}) copy-start(bf16[4,128,8,128]{3,1,0,2:T(8,128)(2,1)} %copy.96) | copy-start | bytes 3145732
  81.9 2.0 copy-start.1
  106.1 32.2 %copy-start.2 = (bf16[8,512,512]{1,2,0:T(8,128)(2,1)S(1)}, bf16[8,512,512]{1,2,0:T(8,128)(2,1)}, u32[]{:S(2)}) copy-start(bf16[8,512,512]{1,2,0:T(8,128)(2,1)} %copy-done.1) | copy-start | bytes 12582916
  140.2 4.8 %copy-start.5 = (bf16[4,128,8,128]{3,1,0,2:T(8,128)(2,1)S(1)}, bf16[4,128,8,128]{3,1,0,2:T(8,128)(2,1)}, u32[]{:S(2)}) copy-start(bf16[4,128,8,128]{3,1,0,2:T(8,128)(2,1)} %copy.99) | copy-start | bytes 3145732
  145.0 2.0 copy-start.8
  145.0 7.1 %copy-start.4 = (bf16[4,128,8,128]{3,1,0,2:T(8,128)(2,1)S(1)}, bf16[4,128,8,128]{3,1,0,2:T(8,128)(2,1)}, u32[]{:S(2)}) copy-start(bf16[4,128,8,128]{3,1,0,2:T(8,128)(2,1)} %copy.96) | copy-start | bytes 3145732
  148.6 29.8 %all-to-all-start.5 = ((bf16[512,8,128]{2,1,0:T(8,128)(2,1)}), bf16[512,8,128]{2,1,0:T(8,128)(2,1)S(1)}, u32[]{:S(2)}, u32[]{:S(2)}) async-start(bf16[512,8,128]{2,1,0:T(8,128)(2,1)} %copy.113), calls=%async_computation.5 | async-start | bytes 2097152 | tf_op jit(solution)/shard_map/all_to_all | solution.py:118
  178.4 30.1 %all-to-all-start.6 = ((bf16[512,8,128]{2,1,0:T(8,128)(2,1)}), bf16[512,8,128]{2,1,0:T(8,128)(2,1)S(1)}, u32[]{:S(2)}, u32[]{:S(2)}) async-start(bf16[512,8,128]{2,1,0:T(8,128)(2,1)} %copy.115), calls=%async_computation.6 | async-start | bytes 2097152 | tf_op jit(solution)/shard_map/all_to_all | solution.py:109
Sparse Core Ops, SparseCore 0:
  11.0 76.0 all-gather.1
Sparse Core Ops, SparseCore 1:
  106.2 155.1 reduce-scatter.1
where the time goes:
time: 271 us
  waiting for transfers between devices  127 us (47%)
  blocking collectives  45.7 us (17%)
  matrix products  32.6 us (12%)
  local copies, waits for them, and re-layouts  23.3 us (9%)
  starting transfers between devices  19.2 us (7%)
  between operations  15.8 us (6%)
  other arithmetic  6.44 us (2%)
    reduce_scatter x1, waiting for transfers between devices, body(): lax.psum_scatter(jnp.einsum('tr,tc->rc', columns, value_low, preferred_el...  51.2 us
    all_to_all x1, blocking collectives, body(): lax.all_to_all(jnp.repeat(value_three, group_size, axis=1), 'seq', split_...  28.8 us
    all_to_all x1, waiting for transfers between devices, body(): lax.all_to_all(query_back, 'seq', split_axis=0, concat_axis=1, tiled=True)  21.1 us
    all_to_all x1, waiting for transfers between devices, body(): lax.all_to_all(key_back.astype(jnp.bfloat16), 'seq', split_axis=0, concat...  18.4 us
    all_to_all x1, blocking collectives, body(): lax.all_to_all(value_back.astype(jnp.bfloat16), 'seq', split_axis=0, conc...  16.9 us
    all_to_all x1, waiting for transfers between devices, body(): lax.all_to_all(query_heads, 'seq', split_axis=1, concat_axis=0, tiled=True)  14.4 us
    all_to_all x1, waiting for transfers between devices, body(): lax.all_to_all(grad_heads, 'seq', split_axis=1, concat_axis=0, tiled=True)  11.8 us
    all_to_all x1, waiting for transfers between devices, body(): lax.all_to_all(jnp.repeat(key_three, group_size, axis=1), 'seq', split_ax...  9.88 us
  transfers between devices with their start and end apart: 7, of which 6 were waited for; matrix products, arithmetic and copies ran while one was open for 22% of the time, Pallas kernels for 0%

commit v1 on v0

--- a/solution.py
+++ b/solution.py
@@ -5,6 +5,22 @@
 
 HD = 128
 far_negative = -1e30
+
+
+def exchange_in_pairs(value, axis, split, join):
+    ways, here = (lax.axis_size(axis), lax.axis_index(axis))
+    width = value.shape[split] // ways
+    shape = list(value.shape)
+    shape[split] = width
+    height = shape[join]
+    shape[join] = height * ways
+    full = jnp.zeros(shape, value.dtype)
+    for mask in range(ways):
+        part = lax.dynamic_slice_in_dim(value, (here ^ mask) * width, width, axis=split)
+        if mask:
+            part = lax.ppermute(part, axis, [(d, d ^ mask) for d in range(ways)])
+        full = lax.dynamic_update_slice_in_dim(full, part, (here ^ mask) * height, axis=join)
+    return full
 
 
 def segment_ids(lengths_row, length):
@@ -89,13 +105,7 @@
     value_three = values.reshape(tokens, kv_heads, HD)
     segment = segment_ids(doc_lengths[0], length)
     key_all, value_all = (
-        lax.all_to_all(
-            jnp.repeat(key_three, group_size, axis=1),
-            "seq",
-            split_axis=1,
-            concat_axis=0,
-            tiled=True,
-        ),
+        exchange_in_pairs(jnp.repeat(key_three, group_size, axis=1), "seq", 1, 0),
         lax.all_to_all(
             jnp.repeat(value_three, group_size, axis=1),
             "seq",

time: 271 us -> 263 us (0.970)
  waiting for transfers between devices: 127 us -> 118 us
    ppermute x0 -> x3, waiting for transfers between devices: none -> 16.2 us  [exchange_in_pairs(): part = lax.ppermute(part, axis, [(d, d ^ mask) for d in range(ways)])]
    all_to_all x1, waiting for transfers between devices: 11.8 us -> 0.01 us  [body(): lax.all_to_all(grad_heads, 'seq', split_axis=1, concat_axis=0, tiled=True)]
    all_to_all x1 -> x0, waiting for transfers between devices: 9.88 us -> none  [body(): lax.all_to_all(jnp.repeat(key_three, group_size, axis=1), 'seq', split_ax...]
    dynamic_update_slice x0 -> x3, local copies, waits for them, and re-layouts: none -> 4.07 us  [exchange_in_pairs(): lax.dynamic_update_slice_in_dim(full, part, (here ^ mask) * height, axis=...]
    all_to_all x1 -> x0, starting transfers between devices: 3.65 us -> none  [body(): lax.all_to_all(jnp.repeat(key_three, group_size, axis=1), 'seq', split_ax...]
    all_to_all x1, waiting for transfers between devices: 14.4 us -> 11.4 us  [body(): lax.all_to_all(query_heads, 'seq', split_axis=1, concat_axis=0, tiled=True)]
    unnamed x22 -> x28, local copies, waits for them, and re-layouts: 6.92 us -> 8.74 us
  transfers between devices with their start and end apart: 7 -> 9, of which waited for: 6 -> 6; matrix products, arithmetic and copies ran while one was open for 22% -> 23% of each run, Pallas kernels for 0% -> 0%
where the time goes in v1:
time: 263 us; the launch traced here: 262 us
  waiting for transfers between devices  118 us (45%)
  blocking collectives  45.7 us (17%)
  matrix products  32.6 us (12%)
  local copies, waits for them, and re-layouts  25.9 us (10%)
  starting transfers between devices  17 us (6%)
  between operations  15.8 us (6%)
  other arithmetic  7.15 us (3%)
    reduce_scatter x1, waiting for transfers between devices, body(): lax.psum_scatter(jnp.einsum('tr,tc->rc', columns, value_low, preferred_el...  51.4 us
    all_to_all x1, blocking collectives, body(): lax.all_to_all(jnp.repeat(value_three, group_size, axis=1), 'seq', split_...  28.8 us
    all_to_all x1, waiting for transfers between devices, body(): lax.all_to_all(query_back, 'seq', split_axis=0, concat_axis=1, tiled=True)  20.4 us
    all_to_all x1, waiting for transfers between devices, body(): lax.all_to_all(key_back.astype(jnp.bfloat16), 'seq', split_axis=0, concat...  18.1 us
    all_to_all x1, blocking collectives, body(): lax.all_to_all(value_back.astype(jnp.bfloat16), 'seq', split_axis=0, conc...  16.9 us
    ppermute x3, waiting for transfers between devices, exchange_in_pairs(): part = lax.ppermute(part, axis, [(d, d ^ mask) for d in range(ways)])  16.2 us
    all_to_all x1, waiting for transfers between devices, body(): lax.all_to_all(query_heads, 'seq', split_axis=1, concat_axis=0, tiled=True)  11.4 us
    unnamed x28, local copies, waits for them, and re-layouts  8.74 us
  transfers between devices with their start and end apart: 9, of which 6 were waited for; matrix products, arithmetic and copies ran while one was open for 23% of the time, Pallas kernels for 0%

profile of v1, /device:TPU:0, one launch (start us, length us, event | category | flops | bytes accessed | tf_op | source)
XLA Modules:
  0.0 262.3 jit_solution(9439346386992776012)
XLA Ops:
  11.7 4.2 %all-to-all-start = ((bf16[128,32,128]{2,0,1:T(8,128)(2,1)}), bf16[128,32,128]{2,0,1:T(8,128)(2,1)S(1)}, u32[]{:S(2)}, u32[]{:S(2)}) async-start(bf16[128,32,128]{2,0,1:T(8,128)(2,1)} %copy.97), calls=%async_computation | async-start | bytes 2097152 | tf_op jit(solution)/shard_map/all_to_all | solution.py:100
  19.0 11.4 %all-to-all-done = bf16[128,32,128]{2,0,1:T(8,128)(2,1)S(1)} async-done(((bf16[128,32,128]{2,0,1:T(8,128)(2,1)}), bf16[128,32,128]{2,0,1:T(8,128)(2,1)S(1)}, u32[]{:S(2)}, u32[]{:S(2)}) %all-to-all-start) | async-done | bytes 1048608 | tf_op jit(solution)/shard_map/all_to_all | solution.py:100
  30.4 3.5 %all-to-all-start.1 = ((bf16[128,32,128]{2,0,1:T(8,128)(2,1)}), bf16[128,32,128]{2,0,1:T(8,128)(2,1)S(1)}, u32[]{:S(2)}, u32[]{:S(2)}) async-start(bf16[128,32,128]{2,0,1:T(8,128)(2,1)} %copy.102), calls=%async_computation.1 | async-start | bytes 2097152 | tf_op jit(solution)/shard_map/all_to_all | solution.py:101
  41.2 13.3 %collective-permute-done.1 = bf16[128,8,128]{0,2,1:T(8,128)(2,1)} collective-permute-done((bf16[128,8,128]{0,2,1:T(8,128)(2,1)}, bf16[128,8,128]{0,2,1:T(8,128)(2,1)}, u32[]{:S(2)}, u32[]{:S(2)}) %collective-permute-start.1) | collective-permute-done | bytes 262176 | tf_op jit(solution)/shard_map/ppermute | solution.py:21
  56.2 2.9 %collective-permute-done.2 = bf16[128,8,128]{0,2,1:T(8,128)(2,1)S(1)} collective-permute-done((bf16[128,8,128]{0,2,1:T(8,128)(2,1)}, bf16[128,8,128]{0,2,1:T(8,128)(2,1)S(1)}, u32[]{:S(2)}, u32[]{:S(2)}) %collective-permute-start.2) | collective-permute-done | bytes 262176 | tf_op jit(solution)/shard_map/ppermute | solution.py:21
  61.0 8.3 %fusion.20 = (f32[8,512]{1,0:T(8,128)S(1)}, f32[8,512,512]{1,2,0:T(8,128)}) fusion(pred[512,512]{0,1:T(8,128)(4,1)S(1)} %copy-done.9, bf16[512,8,128]{0,2,1:T(8,128)(2,1)} %constant_dynamic-update-slice_fusion, bf16[512,8,128]{2,0,1:T(8,128)(2,1)} %bitcast.104), kind=kOutput, calls=%fused_computation.41 | convolution fusion | flops 545260032 | bytes 10764288 | tf_op jit(solution)/shard_map/sub | solution.py:57
  69.3 4.6 %fusion.7 = bf16[8,512,512]{1,2,0:T(8,128)(2,1)S(1)} fusion(f32[8,512,512]{1,2,0:T(8,128)} %get-tuple-element.73, f32[8,512]{1,0:T(8,128)S(1)} %get-tuple-element.72), kind=kLoop, calls=%fused_computation.13 | loop fusion | flops 4194304 | bytes 12599296 | tf_op jit(solution)/shard_map/convert_element_type | solution.py:59
  75.9 16.9 %all_to_all.87 = bf16[512,8,128]{2,1,0:T(8,128)(2,1)S(1)} all-to-all(bf16[512,8,128]{2,1,0:T(8,128)(2,1)S(1)} %copy.105), channel_id=1, replica_groups=mesh['dp'=8,'seq'=4] {'seq'}, dimensions={0} | all-to-all | bytes 2097152 | tf_op jit(solution)/shard_map/all_to_all | solution.py:122
  93.6 4.5 %convolution_bitcast_fusion = f32[4096,512]{0,1:T(8,128)} fusion(bf16[128,512]{0,1:T(8,128)(2,1)S(1)} %bitcast.102, bf16[1,128,4096]{2,1,0:T(8,128)(2,1)S(1)} %copy-done), kind=kOutput, calls=%fused_computation.5 | convolution fusion | flops 536870912 | bytes 9568256 | tf_op jit(solution)/shard_map/tr,tc->rc/dot_general | solution.py:138
  98.2 3.1 %fusion.12 = bf16[16,4,8,128]{3,2,1,0:T(8,128)(2,1)S(1)} fusion(bf16[4096,512]{1,0:T(8,128)(2,1)} %all-gather.2.cloned.1.call-done, bf16[1,128,4096]{2,1,0:T(8,128)(2,1)S(1)} %copy-done), kind=kOutput, calls=%fused_computation.23 | convolution fusion | flops 536936448 | bytes 5373952 | tf_op jit(solution)/shard_map/dot_general | solution.py:92
  101.5 28.8 %all_to_all.88 = bf16[128,32,128]{2,0,1:T(8,128)(2,1)S(1)} all-to-all(bf16[128,32,128]{2,0,1:T(8,128)(2,1)S(1)} %bitcast.93), channel_id=1, replica_groups=mesh['dp'=8,'seq'=4] {'seq'}, dimensions={1} | all-to-all | bytes 2097152 | tf_op jit(solution)/shard_map/all_to_all | solution.py:109
  130.4 1.8 fusion.8
  132.2 4.8 %fusion.1 = bf16[8,512,512]{1,2,0:T(8,128)(2,1)S(1)} fusion(f32[8,512]{1,0:T(8,128)S(1)} %bitcast.111, f32[8,512,512]{1,2,0:T(8,128)} %get-tuple-element.73, f32[8,512]{1,0:T(8,128)S(1)} %get-tuple-element.72, bf16[512,8,128]{2,0,1:T(8,128)(2,1)S(1)} %bitcast.101, bf16[512,8,128]{2,0,1:T(8,128)(2,1)S(1)} %bitcast.99), kind=kOutput, calls=%fused_computation.2 | convolution fusion | flops 545259520 | bytes 14712832 | tf_op jit(solution)/shard_map/ihd,jhd->hij/dot_general | solution.py:64
  137.0 1.9 copy-done.3
  141.1 3.5 %all-to-all-start.4 = ((bf16[512,8,128]{2,1,0:T(8,128)(2,1)}), bf16[512,8,128]{2,1,0:T(8,128)(2,1)S(1)}, u32[]{:S(2)}, u32[]{:S(2)}) async-start(bf16[512,8,128]{2,1,0:T(8,128)(2,1)} %copy.114), calls=%async_computation.4 | async-start | bytes 2097152 | tf_op jit(solution)/shard_map/all_to_all | solution.py:128
  144.7 3.5 %fusion.11 = bf16[512,8,128]{2,0,1:T(8,128)(2,1)S(1)} fusion(bf16[8,512,512]{1,2,0:T(8,128)(2,1)} %copy-done.3, bf16[512,8,128]{2,0,1:T(8,128)(2,1)S(1)} %bitcast.105), kind=kOutput, calls=%fused_computation.21 | convolution fusion | flops 537919488 | bytes 6291456 | tf_op jit(solution)/shard_map/hij,ihd->jhd/dot_general | solution.py:76
  148.2 1.7 copy.116
  149.9 20.4 %all-to-all-done.4 = bf16[512,8,128]{2,1,0:T(8,128)(2,1)S(1)} async-done(((bf16[512,8,128]{2,1,0:T(8,128)(2,1)}), bf16[512,8,128]{2,1,0:T(8,128)(2,1)S(1)}, u32[]{:S(2)}, u32[]{:S(2)}) %all-to-all-start.4) | async-done | bytes 1048608 | tf_op jit(solution)/shard_map/all_to_all | solution.py:128
  170.3 3.5 %all-to-all-start.5 = ((bf16[512,8,128]{2,1,0:T(8,128)(2,1)}), bf16[512,8,128]{2,1,0:T(8,128)(2,1)S(1)}, u32[]{:S(2)}, u32[]{:S(2)}) async-start(bf16[512,8,128]{2,1,0:T(8,128)(2,1)} %copy.116), calls=%async_computation.5 | async-start | bytes 2097152 | tf_op jit(solution)/shard_map/all_to_all | solution.py:119
  173.8 4.7 %fusion.3 = bf16[1,128,4096]{2,1,0:T(8,128)(2,1)} fusion(bf16[128,512]{0,1:T(8,128)(2,1)S(1)} %bitcast.103, bf16[4096,512]{1,0:T(8,128)(2,1)} %all-gather.2.cloned.1.call-done), kind=kOutput, calls=%fused_computation.8 | convolution fusion | flops 537395200 | bytes 5373952 | tf_op jit(solution)/shard_map/tc,rc->tr/dot_general | solution.py:130
  179.7 2.3 broadcast_in_dim_reshape.3
  182.0 18.1 %all-to-all-done.5 = bf16[512,8,128]{2,1,0:T(8,128)(2,1)S(1)} async-done(((bf16[512,8,128]{2,1,0:T(8,128)(2,1)}), bf16[512,8,128]{2,1,0:T(8,128)(2,1)S(1)}, u32[]{:S(2)}, u32[]{:S(2)}) %all-to-all-start.5) | async-done | bytes 1048608 | tf_op jit(solution)/shard_map/all_to_all | solution.py:119
  201.6 51.4 %reduce-scatter.2.cloned.1.call-done = f32[128,512]{0,1:T(8,128)} async-done(((f32[4096,512]{0,1:T(8,128)}), f32[128,512]{0,1:T(8,128)}) %reduce-scatter.2.cloned.1.call-update) | async-done | bytes 262160 | tf_op jit(solution)/shard_map/reduce_scatter | solution.py:137
  253.1 1.8 copy.119
  (64 shorter events, 25.6 us)
Async XLA Ops:
  8.0 85.6 %copy-start = (bf16[1,128,4096]{2,1,0:T(8,128)(2,1)S(1)}, bf16[1,128,4096]{2,1,0:T(8,128)(2,1)}, u32[]{:S(2)}) copy-start(bf16[1,128,4096]{2,1,0:T(8,128)(2,1)} %param.14) | copy-start | bytes 3145732
  8.0 7.9 %copy-start.10 = (bf16[1,128,512]{2,1,0:T(8,128)(2,1)S(1)}, bf16[1,128,512]{2,1,0:T(8,128)(2,1)}, u32[]{:S(2)}) copy-start(bf16[1,128,512]{2,1,0:T(8,128)(2,1)} %param.16) | copy-start | bytes 393220
  8.0 90.1 %all-gather.2.cloned.1.call-start = ((), (), s32[]{:S(2)}) async-start(), calls=%async_computation.7 | async-start | bytes 4718592 | tf_op jit(solution)/shard_map/all_gather | solution.py:133
  11.7 18.7 %all-to-all-start = ((bf16[128,32,128]{2,0,1:T(8,128)(2,1)}), bf16[128,32,128]{2,0,1:T(8,128)(2,1)S(1)}, u32[]{:S(2)}, u32[]{:S(2)}) async-start(bf16[128,32,128]{2,0,1:T(8,128)(2,1)} %copy.97), calls=%async_computation | async-start | bytes 2097152 | tf_op jit(solution)/shard_map/all_to_all | solution.py:100
  17.7 20.6 %copy-start.11 = (s32[1,16]{1,0:T(1,128)S(1)}, s32[1,16]{1,0:T(1,128)}, u32[]{:S(2)}) copy-start(s32[1,16]{1,0:T(1,128)} %param.18) | copy-start | bytes 196
  30.4 30.5 %all-to-all-start.1 = ((bf16[128,32,128]{2,0,1:T(8,128)(2,1)}), bf16[128,32,128]{2,0,1:T(8,128)(2,1)S(1)}, u32[]{:S(2)}, u32[]{:S(2)}) async-start(bf16[128,32,128]{2,0,1:T(8,128)(2,1)} %copy.102), calls=%async_computation.1 | async-start | bytes 2097152 | tf_op jit(solution)/shard_map/all_to_all | solution.py:101
  33.9 219.1 %reduce-scatter.2.cloned.1.call-start = ((), (), s32[]{:S(2)}) async-start(), calls=%async_computation.8 | async-start | bytes 8650752 | tf_op jit(solution)/shard_map/reduce_scatter | solution.py:137
  35.2 1.0 copy-start.6
  36.2 3.4 %collective-permute-start = (bf16[128,8,128]{0,2,1:T(8,128)(2,1)}, bf16[128,8,128]{0,2,1:T(8,128)(2,1)}, u32[]{:S(2)}, u32[]{:S(2)}) collective-permute-start(bf16[128,8,128]{0,2,1:T(8,128)(2,1)} %get-tuple-element.70), channel_id=1, source_target_pairs={{0,1},{1,0},{2,3},{3,2},{4,5},{5,4},{6,7},{7,6},{8,9},{9,8},{10,11... | collective-permute-start | bytes 786440 | tf_op jit(solution)/shard_map/ppermute | solution.py:21
  36.6 17.9 %collective-permute-start.1 = (bf16[128,8,128]{0,2,1:T(8,128)(2,1)}, bf16[128,8,128]{0,2,1:T(8,128)(2,1)}, u32[]{:S(2)}, u32[]{:S(2)}) collective-permute-start(bf16[128,8,128]{0,2,1:T(8,128)(2,1)} %get-tuple-element.69), channel_id=1, source_target_pairs={{0,2},{1,3},{2,0},{3,1},{4,6},{5,7},{6,4},{7,5},{8,10},{9,11},{10,... | collective-permute-start | bytes 786440 | tf_op jit(solution)/shard_map/ppermute | solution.py:21
  38.3 20.8 %collective-permute-start.2 = (bf16[128,8,128]{0,2,1:T(8,128)(2,1)}, bf16[128,8,128]{0,2,1:T(8,128)(2,1)S(1)}, u32[]{:S(2)}, u32[]{:S(2)}) collective-permute-start(bf16[128,8,128]{0,2,1:T(8,128)(2,1)} %get-tuple-element.68), channel_id=1, source_target_pairs={{0,3},{1,2},{2,1},{3,0},{4,7},{5,6},{6,5},{7,4},{8,11},{9,10},{10,... | collective-permute-start | bytes 786440 | tf_op jit(solution)/shard_map/ppermute | solution.py:21
  59.8 1.2 copy-start.9
  61.0 12.9 %copy-start.4 = (bf16[4,128,8,128]{3,1,0,2:T(8,128)(2,1)}, bf16[4,128,8,128]{3,1,0,2:T(8,128)(2,1)S(1)}, u32[]{:S(2)}) copy-start(bf16[4,128,8,128]{3,1,0,2:T(8,128)(2,1)S(1)} %copy.104) | copy-start | bytes 3145732
  73.9 2.0 copy-start.1
  98.1 32.3 %copy-start.5 = (bf16[4,128,8,128]{3,1,0,2:T(8,128)(2,1)S(1)}, bf16[4,128,8,128]{3,1,0,2:T(8,128)(2,1)}, u32[]{:S(2)}) copy-start(bf16[4,128,8,128]{3,1,0,2:T(8,128)(2,1)} %copy-done.4) | copy-start | bytes 3145732
  98.2 32.3 %copy-start.2 = (bf16[8,512,512]{1,2,0:T(8,128)(2,1)S(1)}, bf16[8,512,512]{1,2,0:T(8,128)(2,1)}, u32[]{:S(2)}) copy-start(bf16[8,512,512]{1,2,0:T(8,128)(2,1)} %copy-done.1) | copy-start | bytes 12582916
  132.2 6.7 %copy-start.7 = (bf16[512,8,128]{0,2,1:T(8,128)(2,1)S(1)}, bf16[512,8,128]{0,2,1:T(8,128)(2,1)}, u32[]{:S(2)}) copy-start(bf16[512,8,128]{0,2,1:T(8,128)(2,1)} %constant_dynamic-update-slice_fusion) | copy-start | bytes 3145732
  137.0 1.9 copy-start.3
  139.0 5.7 %copy-start.8 = (bf16[4,128,8,128]{3,1,0,2:T(8,128)(2,1)S(1)}, bf16[4,128,8,128]{3,1,0,2:T(8,128)(2,1)}, u32[]{:S(2)}) copy-start(bf16[4,128,8,128]{3,1,0,2:T(8,128)(2,1)} %copy.99) | copy-start | bytes 3145732
  141.1 29.1 %all-to-all-start.4 = ((bf16[512,8,128]{2,1,0:T(8,128)(2,1)}), bf16[512,8,128]{2,1,0:T(8,128)(2,1)S(1)}, u32[]{:S(2)}, u32[]{:S(2)}) async-start(bf16[512,8,128]{2,1,0:T(8,128)(2,1)} %copy.114), calls=%async_computation.4 | async-start | bytes 2097152 | tf_op jit(solution)/shard_map/all_to_all | solution.py:128
  170.3 29.7 %all-to-all-start.5 = ((bf16[512,8,128]{2,1,0:T(8,128)(2,1)}), bf16[512,8,128]{2,1,0:T(8,128)(2,1)S(1)}, u32[]{:S(2)}, u32[]{:S(2)}) async-start(bf16[512,8,128]{2,1,0:T(8,128)(2,1)} %copy.116), calls=%async_computation.5 | async-start | bytes 2097152 | tf_op jit(solution)/shard_map/all_to_all | solution.py:119
Sparse Core Ops, SparseCore 0:
  11.0 76.0 all-gather.1
Sparse Core Ops, SparseCore 1:
  98.2 154.8 reduce-scatter.1
